TPU v7x, 32 devices: a whole 2x2x4 slice. The times are simulated.
32 devices in a mesh: engine: 4 (over x, core), expert: 8 (over z, y).
Axes of the slice: x: 2, y: 2, z: 4, core: 2. Of those that a mesh axis runs over, the one named last changes fastest.
Arguments:
- tokens: bfloat16 [2, 4096, 4096], P(None, ('engine', 'expert')), may hold values from -6 to 6
- expert_ids: int32 [2, 4096, 2], P(None, ('engine', 'expert')), may hold values from 0 to 7, all different within a row; in each aligned block of 128 rows (0 to 127, 128 to 255, ..., all dimensions but the last counted through in order) at most 48 rows name the same one
- route_gain: float32 [2, 4096, 2], P(None, ('engine', 'expert')), may hold values from 0.1 to 1
- gate_up_master: float32 [8, 4096, 1536], P('expert', 'engine'), may hold values from -0.09375 to 0.09375
- gate_up_moment: float32 [8, 4096, 1536], P('expert', 'engine'), may hold values from -0.09375 to 0.09375
- gate_up_grad: bfloat16 [8, 4096, 1536], P('expert', 'engine'), may hold values from -0.09375 to 0.09375
- down_master: float32 [8, 768, 4096], P('expert', None, 'engine'), may hold values from -0.21875 to 0.21875
- down_moment: float32 [8, 768, 4096], P('expert', None, 'engine'), may hold values from -0.21875 to 0.21875
- down_grad: bfloat16 [8, 768, 4096], P('expert', None, 'engine'), may hold values from -0.21875 to 0.21875
Outputs:
- mixed: bfloat16 [2, 4096, 4096], P(None, ('engine', 'expert'))
Inputs may be any that keep to these rules, and one draw needn't show every extreme that they name: `expert_ids`: in each aligned block of 128 rows of one step, no expert is named by more than 48 rows, a bound that some block reaches; a row names 2 different experts.
All inputs are finite; a program needn't handle non-finite values.
Results may differ from a plain program's by a relative error of at most 0.0081.
Values may be sent and summed in bfloat16 or wider, within the bound.
A program may use at most 128 MiB of HBM per device.

v0:
```python
import jax
import jax.numpy as jnp
from jax import lax
from jax.sharding import PartitionSpec as P


def updated(master, moment, grad):
    return (master - 0.5 * (0.8 * moment + 0.2 * grad.astype(jnp.float32))).astype(jnp.bfloat16)


def per_device(
    tokens,
    expert_ids,
    route_gain,
    gate_up_master,
    gate_up_moment,
    gate_up_grad,
    down_master,
    down_moment,
    down_grad,
):
    steps, row_dev, top_k = expert_ids.shape
    hidden_units = down_master.shape[1]
    experts = gate_up_master.shape[0] * lax.axis_size("expert")
    capacity = 3 * row_dev * top_k // (2 * experts)
    gate_up_weight = updated(gate_up_master, gate_up_moment, gate_up_grad)
    down_weight = updated(down_master, down_moment, down_grad)
    flat_ids = expert_ids.reshape(steps, row_dev * top_k)
    picked = (flat_ids[:, :, None] == jnp.arange(experts, dtype=jnp.int32)[None, None, :]).astype(
        jnp.int32
    )
    earlier = jnp.cumsum(picked, axis=1) - picked
    slot_index = jnp.sum(earlier * picked, axis=2)
    target = (flat_ids * capacity + slot_index).reshape(steps, row_dev, top_k).transpose(0, 2, 1)
    places = jnp.arange(experts * capacity, dtype=jnp.int32)
    matches = target[:, None, :, :] == places[None, :, None, None]
    dispatch_table = jnp.sum(matches.astype(jnp.int32), axis=2).astype(jnp.bfloat16)
    outgoing = jnp.einsum(
        "spr,srd->spd", dispatch_table, tokens, preferred_element_type=jnp.float32
    ).astype(jnp.bfloat16)
    outgoing = outgoing.reshape(steps, experts, capacity, tokens.shape[2])
    received = lax.all_to_all(outgoing, "expert", split_axis=1, concat_axis=2, tiled=True)
    projected = jnp.einsum(
        "tesd,edf->tesf",
        received,
        lax.all_gather(gate_up_weight, "engine", axis=1, tiled=True),
        preferred_element_type=jnp.float32,
    )
    hidden = (jax.nn.silu(projected[..., :hidden_units]) * projected[..., hidden_units:]).astype(
        jnp.bfloat16
    )
    expert_out = jnp.einsum(
        "tesf,efd->tesd",
        hidden,
        lax.all_gather(down_weight, "engine", axis=2, tiled=True),
        preferred_element_type=jnp.float32,
    ).astype(jnp.bfloat16)
    returned = lax.all_to_all(expert_out, "expert", split_axis=2, concat_axis=1, tiled=True)
    returned = returned.reshape(steps, experts * capacity, tokens.shape[2])
    share = (route_gain / jnp.sum(route_gain, axis=2, keepdims=True)).astype(jnp.bfloat16)
    share_by_k = share.transpose(0, 2, 1)[:, None, :, :]
    weighted = jnp.where(matches, share_by_k, jnp.zeros((), jnp.bfloat16))
    combine_table = jnp.sum(weighted.astype(jnp.float32), axis=2).astype(jnp.bfloat16)
    mixed = jnp.einsum("spr,spd->srd", combine_table, returned, preferred_element_type=jnp.float32)
    return mixed.astype(jnp.bfloat16)


def solution(mesh):
    return jax.shard_map(
        per_device,
        mesh=mesh,
        in_specs=(
            P(None, ("engine", "expert"), None),
            P(None, ("engine", "expert"), None),
            P(None, ("engine", "expert"), None),
            P("expert", "engine", None),
            P("expert", "engine", None),
            P("expert", "engine", None),
            P("expert", None, "engine"),
            P("expert", None, "engine"),
            P("expert", None, "engine"),
        ),
        out_specs=P(None, ("engine", "expert"), None),
        check_vma=False,
    )
```

profile of v0, /device:TPU:30, one launch (start us, length us, event | category | flops | bytes accessed | tf_op | source)
XLA Modules:
  0.0 391.8 jit_solution(7161549556185049406)
XLA Ops:
  6.5 0.0 copy-start
  6.5 0.0 all-gather.5.cloned.1.call-start
  6.5 6.7 %copy.70 = f32[1,1024,1536]{1,2,0:T(8,128)} copy(f32[1,1024,1536]{2,1,0:T(8,128)} %param.13) | data formatting | bytes 12582912 | tf_op args[4]
  13.2 6.6 %copy.72 = f32[1,1024,1536]{1,2,0:T(8,128)} copy(f32[1,1024,1536]{2,1,0:T(8,128)} %param.12) | data formatting | bytes 12582912 | tf_op args[3]
  19.8 4.6 %copy.71 = bf16[1,1024,1536]{1,2,0:T(8,128)(2,1)} copy(bf16[1,1024,1536]{2,1,0:T(8,128)(2,1)} %param.14) | data formatting | bytes 6291456 | tf_op args[5]
  24.5 0.0 copy-start.2
  24.5 9.1 %subtract_convert_fusion = bf16[1,1024,1536]{1,2,0:T(8,128)(2,1)} fusion(f32[1,1024,1536]{1,2,0:T(8,128)} %copy.72, bf16[1,1024,1536]{1,2,0:T(8,128)(2,1)} %copy.71, f32[1,1024,1536]{1,2,0:T(8,128)} %copy.70), kind=kLoop, calls=%fused_computation.9 | loop fusion | flops 11010048 | bytes 18874368 | tf_op jit(solution)/shard_map/convert_element_type | solution.py:8
  33.6 0.0 all-gather.5.cloned.1.call-update
  33.6 0.0 copy-done.2
  33.6 0.1 copy.64
  33.7 0.1 eq.42
  33.9 0.1 eq.38
  34.0 1.2 reduce-window.6
  35.2 0.2 slice_reduce_fusion
  35.4 0.1 fusion.26
  35.5 0.1 reduce_sum.42
  35.7 0.1 copy.66
  35.8 0.1 convert_reduce_fusion
  35.9 0.0 copy-done
  35.9 1.8 convolution_convert_fusion
  37.7 3.1 copy.73
  40.8 6.0 %all-to-all-start = ((bf16[2,8,48,4096]{3,2,0,1:T(8,128)(2,1)}), bf16[2,8,48,4096]{3,2,0,1:T(8,128)(2,1)}, u32[]{:S(2)}, u32[]{:S(2)}) async-start(bf16[2,8,48,4096]{3,2,0,1:T(8,128)(2,1)} %copy.73), calls=%async_computation | async-start | bytes 12582912 | tf_op jit(solution)/shard_map/all_to_all | solution.py:42
  46.8 0.0 all-gather.3.cloned.1.call-start
  46.8 4.5 %copy.67 = f32[1,768,1024]{1,2,0:T(8,128)} copy(f32[1,768,1024]{2,1,0:T(8,128)} %param.16) | data formatting | bytes 6291456 | tf_op args[7]
  51.3 3.6 copy.69
  54.9 1.7 copy.68
  56.6 4.7 %subtract_convert_fusion.1 = bf16[1,768,1024]{1,2,0:T(8,128)(2,1)} fusion(f32[1,768,1024]{1,2,0:T(8,128)} %copy.69, bf16[1,768,1024]{1,2,0:T(8,128)(2,1)S(1)} %copy.68, f32[1,768,1024]{1,2,0:T(8,128)} %copy.67), kind=kLoop, calls=%fused_computation.13 | loop fusion | flops 5505024 | bytes 9437184 | tf_op jit(solution)/shard_map/convert_element_type | solution.py:8
  61.3 0.0 all-gather.3.cloned.1.call-update
  61.3 121.4 %all-to-all-done = bf16[2,8,48,4096]{3,2,0,1:T(8,128)(2,1)} async-done(((bf16[2,8,48,4096]{3,2,0,1:T(8,128)(2,1)}), bf16[2,8,48,4096]{3,2,0,1:T(8,128)(2,1)}, u32[]{:S(2)}, u32[]{:S(2)}) %all-to-all-start) | async-done | bytes 6291488 | tf_op jit(solution)/shard_map/all_to_all | solution.py:42
  182.7 6.3 %copy.74 = bf16[2,8,48,4096]{3,2,1,0:T(8,128)(2,1)} copy(bf16[2,8,48,4096]{3,2,0,1:T(8,128)(2,1)} %all-to-all-done) | data formatting | bytes 12582912 | tf_op jit(solution)/shard_map/all_to_all | solution.py:42
  189.0 0.0 all-gather.5.cloned.1.call-done
  189.0 15.6 %fusion.13 = f32[2,1,384,1536]{2,3,0,1:T(8,128)} fusion(bf16[2,384,4096]{2,1,0:T(8,128)(2,1)} %bitcast.47, bf16[1,4096,1536]{1,2,0:T(8,128)(2,1)} %all-gather.5.cloned.1.call-done), kind=kOutput, calls=%fused_computation.12 | convolution fusion | flops 9663676416 | bytes 23592960 | tf_op jit(solution)/shard_map/tesd,edf->tesf/dot_general | solution.py:43
  204.6 0.0 all-gather.3.cloned.1.call-done
  204.6 10.6 %fusion.7 = bf16[2,1,384,4096]{2,3,0,1:T(8,128)(2,1)} fusion(bf16[1,768,4096]{1,2,0:T(8,128)(2,1)} %all-gather.3.cloned.1.call-done, f32[2,1,384,1536]{2,3,0,1:T(8,128)} %fusion.13), kind=kOutput, calls=%fused_computation.10 | convolution fusion | flops 4838522880 | bytes 17301504 | tf_op jit(solution)/shard_map/tesf,efd->tesd/dot_general | solution.py:52
  215.1 16.2 %copy.76 = bf16[2,1,384,4096]{3,0,1,2:T(2,128)(2,1)} copy(bf16[2,1,384,4096]{2,3,0,1:T(8,128)(2,1)} %fusion.7) | data formatting | bytes 12582912 | tf_op jit(solution)/shard_map/convert_element_type | solution.py:57
  231.4 0.0 copy-start.3
  231.4 7.1 %all-to-all-start.1 = ((bf16[2,1,384,4096]{3,0,1,2:T(2,128)(2,1)}), bf16[2,1,384,4096]{3,0,1,2:T(2,128)(2,1)}, u32[]{:S(2)}, u32[]{:S(2)}) async-start(bf16[2,1,384,4096]{3,0,1,2:T(2,128)(2,1)} %copy.76), calls=%async_computation.1 | async-start | bytes 12582912 | tf_op jit(solution)/shard_map/all_to_all | solution.py:58
  238.5 0.0 copy-done.3
  238.5 0.0 copy-start.1
  238.5 0.1 fusion.23
  238.6 134.9 %all-to-all-done.1 = bf16[2,1,384,4096]{3,0,1,2:T(2,128)(2,1)} async-done(((bf16[2,1,384,4096]{3,0,1,2:T(2,128)(2,1)}), bf16[2,1,384,4096]{3,0,1,2:T(2,128)(2,1)}, u32[]{:S(2)}, u32[]{:S(2)}) %all-to-all-start.1) | async-done | bytes 6291488 | tf_op jit(solution)/shard_map/all_to_all | solution.py:58
  373.5 11.4 %fusion.10 = bf16[2,128,4096]{2,1,0:T(8,128)(2,1)} fusion(bf16[2,384,128]{2,1,0:T(8,128)(2,1)S(1)} %fusion.23, bf16[2,1,384,4096]{3,0,1,2:T(2,128)(2,1)} %all-to-all-done.1), kind=kOutput, calls=%fused_computation.11 | convolution fusion | flops 806354944 | bytes 8585216 | tf_op jit(solution)/shard_map/spr,spd->srd/dot_general | solution.py:64
  385.0 0.0 copy-done.1
  (5 shorter events, 0.1 us)
Async XLA Ops:
  6.5 29.4 %copy-start = (bf16[2,128,4096]{2,1,0:T(8,128)(2,1)S(1)}, bf16[2,128,4096]{2,1,0:T(8,128)(2,1)}, u32[]{:S(2)}) copy-start(bf16[2,128,4096]{2,1,0:T(8,128)(2,1)} %param.9) | copy-start | bytes 6291460
  6.5 182.5 %all-gather.5.cloned.1.call-start = ((), (), s32[]{:S(2)}) async-start(), calls=%async_computation.3 | async-start | bytes 15728640 | tf_op jit(solution)/shard_map/all_gather | solution.py:46
  24.5 9.1 %copy-start.2 = (s32[2,128,2]{1,2,0:T(2,128)S(1)}, s32[2,128,2]{1,2,0:T(2,128)}, u32[]{:S(2)}) copy-start(s32[2,128,2]{1,2,0:T(2,128)} %param.10) | copy-start | bytes 6148
  40.8 141.9 %all-to-all-start = ((bf16[2,8,48,4096]{3,2,0,1:T(8,128)(2,1)}), bf16[2,8,48,4096]{3,2,0,1:T(8,128)(2,1)}, u32[]{:S(2)}, u32[]{:S(2)}) async-start(bf16[2,8,48,4096]{3,2,0,1:T(8,128)(2,1)} %copy.73), calls=%async_computation | async-start | bytes 12582912 | tf_op jit(solution)/shard_map/all_to_all | solution.py:42
  46.8 157.7 %all-gather.3.cloned.1.call-start = ((), (), s32[]{:S(2)}) async-start(), calls=%async_computation.2 | async-start | bytes 7864320 | tf_op jit(solution)/shard_map/all_gather | solution.py:55
  231.4 7.2 %copy-start.3 = (f32[2,128,2]{1,2,0:T(2,128)S(1)}, f32[2,128,2]{1,2,0:T(2,128)}, u32[]{:S(2)}) copy-start(f32[2,128,2]{1,2,0:T(2,128)} %param.11) | copy-start | bytes 6148
  231.4 142.2 %all-to-all-start.1 = ((bf16[2,1,384,4096]{3,0,1,2:T(2,128)(2,1)}), bf16[2,1,384,4096]{3,0,1,2:T(2,128)(2,1)}, u32[]{:S(2)}, u32[]{:S(2)}) async-start(bf16[2,1,384,4096]{3,0,1,2:T(2,128)(2,1)} %copy.76), calls=%async_computation.1 | async-start | bytes 12582912 | tf_op jit(solution)/shard_map/all_to_all | solution.py:58
  238.5 146.5 %copy-start.1 = (bf16[2,128,4096]{2,1,0:T(8,128)(2,1)S(1)}, bf16[2,128,4096]{2,1,0:T(8,128)(2,1)}, u32[]{:S(2)}) copy-start(bf16[2,128,4096]{2,1,0:T(8,128)(2,1)} %param.9) | copy-start | bytes 6291460
Sparse Core Ops, SparseCore 0:
  33.7 82.0 all-gather.4
  117.4 46.3 all-gather.2
where the time goes:
time: 396 us; the launch traced here: 392 us
  waiting for transfers between devices  256 us (65%)
  local copies, waits for them, and re-layouts  54.2 us (14%)
  matrix products  39.4 us (10%)
  other arithmetic  15.3 us (4%)
  between operations  13.5 us (3%)
  starting transfers between devices  13.2 us (3%)
    all_to_all x1, waiting for transfers between devices, per_device(): lax.all_to_all(expert_out, 'expert', split_axis=2, concat_axis=1, tiled=T...  135 us
    all_to_all x1, waiting for transfers between devices, per_device(): lax.all_to_all(outgoing, 'expert', split_axis=1, concat_axis=2, tiled=True)  121 us
    unnamed x15, local copies, waits for them, and re-layouts  27.8 us
    convert_element_type x1, local copies, waits for them, and re-layouts, per_device(): expert_out = jnp.einsum('tesf,efd->tesd', hidden, lax.all_gather(down_wei...  16.2 us
    dot_general x1, matrix products, per_device(): jnp.einsum('tesd,edf->tesf', received, lax.all_gather(gate_up_weight, 'en...  15.6 us
    convert_element_type x2, other arithmetic, updated(): (master - 0.5 * (0.8 * moment + 0.2 * grad.astype(jnp.float32))).astype(j...  13.8 us
    dot_general x1, matrix products, per_device(): jnp.einsum('spr,spd->srd', combine_table, returned, preferred_element_typ...  11.4 us
    dot_general x1, matrix products, per_device(): jnp.einsum('tesf,efd->tesd', hidden, lax.all_gather(down_weight, 'engine'...  10.6 us
  transfers between devices with their start and end apart: 4, of which 2 were waited for; matrix products, arithmetic and copies ran while one was open for 11% of the time, Pallas kernels for 0%

commit v1 on v0

v1 whole, which is shorter than its diff:
```python
import functools

import jax
import jax.numpy as jnp
from jax import lax
from jax.experimental import pallas as pl
from jax.experimental.pallas import tpu as pltpu
from jax.sharding import PartitionSpec as P

MESH = pl.DeviceIdType.MESH
TILE = 512


def updated(master, moment, grad):
    return (master - 0.5 * (0.8 * moment + 0.2 * grad.astype(jnp.float32))).astype(jnp.bfloat16)


def layer_kernel(
    n_engine,
    n_expert,
    cap,
    tokens,
    near_tab,
    far_tab,
    gu_master,
    gu_moment,
    gu_grad,
    dn_master,
    dn_moment,
    dn_grad,
    mixed,
    gate_up,
    down,
    own_rows,
    far_rows,
    relay_tab,
    near_send,
    far_send,
    slots,
    hidden,
    near_back,
    far_back,
    part_send,
    part_recv,
    gu_stage,
    gu_grad_stage,
    dn_stage,
    dn_grad_stage,
    local_sem,
    stage_sem,
    token_send,
    token_recv,
    slot_send,
    slot_recv,
    weight_send,
    weight_recv,
):
    half = n_expert // 2
    pairs = n_engine // 2
    steps, rows, width = own_rows.shape
    places = half * cap
    ff = down.shape[0]
    g, e = lax.axis_index("engine"), lax.axis_index("expert")
    core, pair = lax.rem(g, 2), g // 2
    side, me = e // half, lax.rem(e, half)
    partner = (g, lax.rem(e + half, n_expert))
    sibling = (pair * 2 + 1 - core, e)

    def near(j):
        return lax.rem(me + j, half)

    def near_device(j):
        return (g, side * half + near(j))

    def same_core(q):
        return (lax.rem(pair + q, pairs) * 2 + core, e)

    def seats(index, base=0):
        return pl.ds(pl.multiple_of(base + index * cap, 16), cap)

    sends = []

    def send(src, dst, send_sem, recv_sem, device):
        copy = pltpu.make_async_remote_copy(
            src_ref=src, dst_ref=dst, send_sem=send_sem, recv_sem=recv_sem,
            device_id=device, device_id_type=MESH,
        )
        copy.start()
        sends.append(copy)

    def arrive(dst, send_sem, recv_sem, device):
        pltpu.make_async_remote_copy(
            src_ref=dst, dst_ref=dst, send_sem=send_sem, recv_sem=recv_sem,
            device_id=device, device_id_type=MESH,
        ).wait_recv()

    peers = [partner, sibling]
    peers += [near_device(j) for j in range(1, half)]
    peers += [same_core(q) for q in range(1, pairs)]
    barrier = pltpu.get_barrier_semaphore()
    for device in peers:
        pl.semaphore_signal(barrier, inc=1, device_id=device, device_id_type=MESH)
    pl.semaphore_wait(barrier, len(peers))

    send(far_tab, relay_tab, token_send.at[2 * steps], token_recv.at[2 * steps], partner)
    for s in range(steps):
        send(tokens.at[s], far_rows.at[s], token_send.at[s], token_recv.at[s], partner)
    own_copy = pltpu.make_async_copy(tokens, own_rows, local_sem.at[4 * steps])
    own_copy.start()

    gu_rows, dn_cols = gu_master.shape[1], dn_master.shape[2]
    gu_chunk, dn_chunk = gu_stage.shape[2], dn_stage.shape[2]
    n_gu, n_dn = gu_rows // gu_chunk, ff // dn_chunk
    chunks = n_gu + n_dn

    def weight_part(c, owner):
        if c < n_gu:
            start = pl.multiple_of(owner * gu_rows + c * gu_chunk, 16)
            return gate_up.at[pl.ds(start, gu_chunk)]
        columns = pl.ds(pl.multiple_of(owner * dn_cols, 128), dn_cols)
        return down.at[pl.ds((c - n_gu) * dn_chunk, dn_chunk), columns]

    def staged(c):
        slot = c % 2
        if c < n_gu:
            part = pl.ds(c * gu_chunk, gu_chunk)
            refs = (gu_master, gu_moment, gu_grad)
            stages = (gu_stage.at[slot, 0], gu_stage.at[slot, 1], gu_grad_stage.at[slot])
        else:
            part = pl.ds((c - n_gu) * dn_chunk, dn_chunk)
            refs = (dn_master, dn_moment, dn_grad)
            stages = (dn_stage.at[slot, 0], dn_stage.at[slot, 1], dn_grad_stage.at[slot])
        return [
            pltpu.make_async_copy(ref.at[0, part], stage, stage_sem.at[c, i])
            for i, (ref, stage) in enumerate(zip(refs, stages))
        ]

    for copy in staged(0):
        copy.start()
    for c in range(chunks):
        if c + 1 < chunks:
            for copy in staged(c + 1):
                copy.start()
        for copy in staged(c):
            copy.wait()
        slot = c % 2
        mine = weight_part(c, g)
        if c < n_gu:
            mine[...] = updated(gu_stage[slot, 0], gu_stage[slot, 1], gu_grad_stage[slot])
        else:
            mine[...] = updated(dn_stage[slot, 0], dn_stage[slot, 1], dn_grad_stage[slot])
        for q in range(1, pairs):
            send(mine, mine, weight_send.at[c, q], weight_recv.at[c, q], same_core(q))
        send(mine, mine, weight_send.at[c, 0], weight_recv.at[c, 0], sibling)

    def relay(c):
        for q in range(1, pairs):
            owner = lax.rem(pair - q + pairs, pairs) * 2 + core
            part = weight_part(c, owner)
            arrive(part, weight_send.at[c, q], weight_recv.at[c, q], sibling)
            k = pairs + q - 1
            send(part, part, weight_send.at[c, k], weight_recv.at[c, k], sibling)

    def relayed(c):
        arrive(weight_part(c, g + 1 - 2 * core), weight_send.at[c, 0], weight_recv.at[c, 0], sibling)
        for q in range(1, pairs):
            owner = lax.rem(pair - q + pairs, pairs) * 2 + 1 - core
            k = pairs + q - 1
            arrive(weight_part(c, owner), weight_send.at[c, k], weight_recv.at[c, k], sibling)

    def hand_out(s, kind, table, source, outgoing):
        @pl.loop(0, width // TILE)
        def _(t):
            columns = pl.ds(pl.multiple_of(t * TILE, TILE), TILE)
            outgoing[s, :, columns] = jnp.dot(
                table[s, 0], source[s, :, columns], preferred_element_type=jnp.float32
            ).astype(jnp.bfloat16)

        base = kind * places
        for j in range(1, half):
            send(
                outgoing.at[s, seats(near(j))], slots.at[s, seats(me, base)],
                slot_send.at[kind, s, j], slot_recv.at[kind, s, j], near_device(j),
            )
        keep = pltpu.make_async_copy(
            outgoing.at[s, seats(me)], slots.at[s, seats(me, base)], local_sem.at[kind * steps + s]
        )
        keep.start()
        return keep

    own_copy.wait()
    kept = {}
    for s in range(steps):
        kept[0, s] = hand_out(s, 0, near_tab, own_rows, near_send)
    arrive(relay_tab, token_send.at[2 * steps], token_recv.at[2 * steps], partner)
    for s in range(steps):
        arrive(far_rows.at[s], token_send.at[s], token_recv.at[s], partner)
        kept[1, s] = hand_out(s, 1, relay_tab, far_rows, far_send)
        for c in range(s * n_gu // steps, (s + 1) * n_gu // steps):
            relay(c)
    for c in range(n_gu):
        relayed(c)

    def project(s):
        for kind in range(2):
            kept[kind, s].wait()
            for j in range(1, half):
                origin = lax.rem(me - j + half, half)
                arrive(
                    slots.at[s, seats(origin, kind * places)],
                    slot_send.at[kind, s, j], slot_recv.at[kind, s, j], near_device(j),
                )

        @pl.loop(0, ff // 256)
        def _(t):
            left = pl.ds(pl.multiple_of(t * 256, 256), 256)
            right = pl.ds(pl.multiple_of(ff + t * 256, 256), 256)
            gate = jnp.dot(slots[s], gate_up[:, left], preferred_element_type=jnp.float32)
            up = jnp.dot(slots[s], gate_up[:, right], preferred_element_type=jnp.float32)
            hidden[s, :, left] = (gate / (1.0 + jnp.exp(-gate)) * up).astype(jnp.bfloat16)

    def expand(s):
        @pl.loop(0, width // TILE)
        def _(t):
            columns = pl.ds(pl.multiple_of(t * TILE, TILE), TILE)
            slots[s, :, columns] = jnp.dot(
                hidden[s], down[:, columns], preferred_element_type=jnp.float32
            ).astype(jnp.bfloat16)

        for kind, back in ((1, far_back), (0, near_back)):
            for j in range(1, half):
                send(
                    slots.at[s, seats(near(j), kind * places)], back.at[s, seats(me)],
                    slot_send.at[2 + kind, s, j], slot_recv.at[2 + kind, s, j], near_device(j),
                )
            keep = pltpu.make_async_copy(
                slots.at[s, seats(me, kind * places)], back.at[s, seats(me)],
                local_sem.at[(2 + kind) * steps + s],
            )
            keep.start()
            kept[2 + kind, s] = keep

    def back_here(s, kind, back):
        kept[2 + kind, s].wait()
        for j in range(1, half):
            origin = lax.rem(me - j + half, half)
            arrive(
                back.at[s, seats(origin)],
                slot_send.at[2 + kind, s, j], slot_recv.at[2 + kind, s, j], near_device(j),
            )

    def weighted(table, s, back, columns):
        return lax.dot_general(
            table[s, 1], back[s, :, columns], (((0,), (0,)), ((), ())),
            preferred_element_type=jnp.float32,
        )

    for s in range(steps):
        project(s)
        if s == 0:
            for c in range(n_gu, chunks):
                relay(c)
            for c in range(n_gu, chunks):
                relayed(c)
        expand(s)

    for s in range(steps):
        back_here(s, 1, far_back)

        @pl.loop(0, width // TILE)
        def _(t):
            columns = pl.ds(pl.multiple_of(t * TILE, TILE), TILE)
            part_send[s, :, columns] = weighted(relay_tab, s, far_back, columns).astype(jnp.bfloat16)

        send(
            part_send.at[s], part_recv.at[s],
            token_send.at[steps + s], token_recv.at[steps + s], partner,
        )

    for s in range(steps):
        back_here(s, 0, near_back)
        arrive(part_recv.at[s], token_send.at[steps + s], token_recv.at[steps + s], partner)

        @pl.loop(0, width // TILE)
        def _(t):
            columns = pl.ds(pl.multiple_of(t * TILE, TILE), TILE)
            total = weighted(near_tab, s, near_back, columns)
            total = total + part_recv[s, :, columns].astype(jnp.float32)
            mixed[s, :, columns] = total.astype(jnp.bfloat16)

    for copy in sends:
        copy.wait_send()


def per_device(
    tokens,
    expert_ids,
    route_gain,
    gate_up_master,
    gate_up_moment,
    gate_up_grad,
    down_master,
    down_moment,
    down_grad,
):
    steps, rows, top_k = expert_ids.shape
    width = tokens.shape[2]
    n_engine, n_expert = lax.axis_size("engine"), lax.axis_size("expert")
    half, pairs = n_expert // 2, n_engine // 2
    cap = 3 * rows * top_k // (2 * n_expert)
    cap = -(-cap // 16) * 16
    places = half * cap
    ff = down_master.shape[1]

    named = expert_ids[:, None, :, :] == jnp.arange(n_expert, dtype=jnp.int32)[None, :, None, None]
    share = (route_gain / jnp.sum(route_gain, axis=2, keepdims=True)).astype(jnp.bfloat16)
    chosen = jnp.any(named, axis=3)
    portion = jnp.sum(jnp.where(named, share[:, None].astype(jnp.float32), 0.0), axis=3)
    ahead = jnp.arange(rows)[:, None] < jnp.arange(rows)[None, :]
    place = jnp.einsum(
        "ser,rq->seq", chosen.astype(jnp.bfloat16), ahead.astype(jnp.bfloat16),
        preferred_element_type=jnp.float32,
    ).astype(jnp.int32)
    match = chosen[:, :, None, :] & (
        place[:, :, None, :] == jnp.arange(cap, dtype=jnp.int32)[None, None, :, None]
    )
    table = jnp.stack(
        [match.astype(jnp.bfloat16), jnp.where(match, portion[:, :, None, :], 0.0).astype(jnp.bfloat16)],
        axis=1,
    ).reshape(steps, 2, 2, places, rows)
    side = lax.axis_index("expert") // half
    near_tab = lax.dynamic_index_in_dim(table, side, 2, keepdims=False)
    far_tab = lax.dynamic_index_in_dim(table, 1 - side, 2, keepdims=False)

    gu_rows, dn_cols = gate_up_master.shape[1], down_master.shape[2]
    gu_chunk, dn_chunk = min(128, gu_rows), ff // 4
    chunks = gu_rows // gu_chunk + 4
    bf16, f32 = jnp.bfloat16, jnp.float32
    dma = pltpu.SemaphoreType.DMA
    hbm, vmem = pl.BlockSpec(memory_space=pl.ANY), pl.BlockSpec(memory_space=pltpu.VMEM)
    return pl.pallas_call(
        functools.partial(layer_kernel, n_engine, n_expert, cap),
        out_shape=jax.ShapeDtypeStruct(tokens.shape, bf16),
        in_specs=[hbm, vmem, vmem] + [hbm] * 6,
        out_specs=vmem,
        scratch_shapes=[
            pltpu.VMEM((width, 2 * ff), bf16),
            pltpu.VMEM((ff, width), bf16),
            pltpu.VMEM((steps, rows, width), bf16),
            pltpu.VMEM((steps, rows, width), bf16),
            pltpu.VMEM((steps, 2, places, rows), bf16),
            pltpu.VMEM((steps, places, width), bf16),
            pltpu.VMEM((steps, places, width), bf16),
            pltpu.VMEM((steps, 2 * places, width), bf16),
            pltpu.VMEM((steps, 2 * places, ff), bf16),
            pltpu.VMEM((steps, places, width), bf16),
            pltpu.VMEM((steps, places, width), bf16),
            pltpu.VMEM((steps, rows, width), bf16),
            pltpu.VMEM((steps, rows, width), bf16),
            pltpu.VMEM((2, 2, gu_chunk, 2 * ff), f32),
            pltpu.VMEM((2, gu_chunk, 2 * ff), bf16),
            pltpu.VMEM((2, 2, dn_chunk, dn_cols), f32),
            pltpu.VMEM((2, dn_chunk, dn_cols), bf16),
            dma((4 * steps + 1,)),
            dma((chunks, 3)),
            dma((2 * steps + 1,)),
            dma((2 * steps + 1,)),
            dma((4, steps, half)),
            dma((4, steps, half)),
            dma((chunks, 2 * pairs - 1)),
            dma((chunks, 2 * pairs - 1)),
        ],
        compiler_params=pltpu.CompilerParams(
            collective_id=0, has_side_effects=True, vmem_limit_bytes=63 * 1024 * 1024
        ),
    )(
        tokens, near_tab, far_tab, gate_up_master, gate_up_moment, gate_up_grad,
        down_master, down_moment, down_grad,
    )


def solution(mesh):
    return jax.shard_map(
        per_device,
        mesh=mesh,
        in_specs=(
            P(None, ("engine", "expert"), None),
            P(None, ("engine", "expert"), None),
            P(None, ("engine", "expert"), None),
            P("expert", "engine", None),
            P("expert", "engine", None),
            P("expert", "engine", None),
            P("expert", None, "engine"),
            P("expert", None, "engine"),
            P("expert", None, "engine"),
        ),
        out_specs=P(None, ("engine", "expert"), None),
        check_vma=False,
    )
```

time: 396 us -> 265 us (0.67)
  the two profiles are of different devices: /device:TPU:30 before, /device:TPU:5 now
where the time goes in v1:
time: 265 us
  Pallas kernels  258 us (97%)
  local copies, waits for them, and re-layouts  4.09 us (2%)
    pallas_call x1, Pallas kernels, per_device(): pl.pallas_call(functools.partial(layer_kernel, n_engine, n_expert, cap),...  258 us

profile of v1, /device:TPU:5, one launch (start us, length us, event | category | flops | bytes accessed | tf_op | source)
XLA Modules:
  0.0 265.2 jit_solution(9493627420534982901)
XLA Ops:
  0.0 0.7 fusion.8
  0.7 0.8 fusion.3
  1.5 0.7 select_reduce_fusion
  2.2 0.1 eq.51
  2.2 0.1 convolution_convert_fusion
  2.5 0.2 select_convert_fusion
  2.8 0.8 copy_bitcast_fusion
  3.6 258.5 %shard_map.91 = bf16[2,128,4096]{2,1,0:T(8,128)(2,1)} custom-call(bf16[2,128,4096]{2,1,0:T(8,128)(2,1)} %tokens.1, bf16[2,2,192,128]{3,2,1,0:T(8,128)(2,1)} %get-tuple-element.10.near_tab, bf16[2,2,192,128]{3,2,1,0:T(8,128)(2,1)} %get-tuple-element.9.far_tab, f32[1,1024,1536]{2,1,0:T(8,128)} %gu_master.1, f32[1,1024,1536]{2,1,0:T(8,128)} %gu_moment.1, ...), custom_call_target="tpu_custom_call" | custom-call | tf_op jit(solution)/shard_map/pallas_call | solution.py:341
  262.1 3.1 %copy.21 = bf16[2,128,4096]{2,1,0:T(8,128)(2,1)} copy(bf16[2,128,4096]{2,1,0:T(8,128)(2,1)} %shard_map.91) | data formatting | bytes 4194304
  (6 shorter events, 0.2 us)

commit v2 on v1

v2 whole, which is shorter than its diff:
```python
import functools

import jax
import jax.numpy as jnp
from jax import lax
from jax.experimental import pallas as pl
from jax.experimental.pallas import tpu as pltpu
from jax.sharding import PartitionSpec as P

MESH = pl.DeviceIdType.MESH
TILE = 512


def updated(master, moment, grad):
    return (master - 0.5 * (0.8 * moment + 0.2 * grad.astype(jnp.float32))).astype(jnp.bfloat16)


def layer_kernel(
    n_engine,
    n_expert,
    cap,
    tokens,
    near_tab,
    far_tab,
    gu_master,
    gu_moment,
    gu_grad,
    dn_master,
    dn_moment,
    dn_grad,
    mixed,
    gate_up,
    down,
    far_rows,
    relay_tab,
    near_send,
    far_send,
    slots,
    hidden,
    near_back,
    far_back,
    part_recv,
    gu_stage,
    gu_grad_stage,
    dn_stage,
    dn_grad_stage,
    token_sem,
    stage_sem,
    tab_send,
    tab_recv,
    row_send,
    row_recv,
    near_out_send,
    near_out_recv,
    far_out_send,
    far_out_recv,
    near_back_send,
    near_back_recv,
    far_back_send,
    far_back_recv,
    part_send_sem,
    part_recv_sem,
    weight_send,
    weight_recv,
):
    half = n_expert // 2
    lines = half // 2
    pairs = n_engine // 2
    steps, rows, width = mixed.shape
    places = half * cap
    ff = down.shape[0]
    group = width // pairs
    tile = min(TILE, group)
    g, e = lax.axis_index("engine"), lax.axis_index("expert")
    core, pair = lax.rem(g, 2), g // 2
    side, me = e // half, lax.rem(e, half)
    line, inner = lax.rem(me, lines), me // lines
    lands = inner != side
    landing = (g, (1 - side) * half + side * lines + line)
    sibling = (pair * 2 + 1 - core, e)

    def near(j):
        return lax.rem(me + j, half)

    def near_device(index):
        return (g, side * half + index)

    def lander(y):
        return (1 - side) * lines + y

    def source_device(b):
        return (g, (1 - side) * half + b * lines + line)

    def same_core(q):
        return (lax.rem(pair + q, pairs) * 2 + core, e)

    def seats(index, base=0):
        return pl.ds(pl.multiple_of(base + index * cap, 16), cap)

    def columns_of(q):
        start = lax.rem(pair - q + pairs, pairs) * group
        return pl.ds(pl.multiple_of(start, 128), group)

    def tile_of(q, t):
        start = lax.rem(pair - q + pairs, pairs) * group + t * tile
        return pl.ds(pl.multiple_of(start, 128), tile)

    def remote(src, dst, send_sem, recv_sem, device):
        return pltpu.make_async_remote_copy(
            src_ref=src, dst_ref=dst, send_sem=send_sem, recv_sem=recv_sem,
            device_id=device, device_id_type=MESH,
        )

    sends, landing_sends, guarded_sends = [], [], []

    def send(*args):
        copy = remote(*args)
        copy.start()
        sends.append(copy)

    def arrive(dst, sem):
        remote(dst, dst, tab_send.at[0], sem, sibling).wait_recv()

    peers = [landing, (g, (1 - side) * half + (1 - side) * lines + line), sibling]
    peers += [near_device(near(j)) for j in range(1, half)]
    peers += [same_core(q) for q in range(1, pairs)]
    barrier = pltpu.get_barrier_semaphore()
    for device in peers:
        pl.semaphore_signal(barrier, inc=1, device_id=device, device_id_type=MESH)

    pl.semaphore_wait(barrier, len(peers))

    send(far_tab, relay_tab.at[inner], tab_send.at[0], tab_recv.at[inner], landing)
    for s in range(steps):
        send(
            tokens.at[s], far_rows.at[inner, s], row_send.at[s], row_recv.at[inner, s], landing
        )
    own_copy = pltpu.make_async_copy(tokens, mixed, token_sem.at[0])
    own_copy.start()

    gu_rows, dn_cols = gu_master.shape[1], dn_master.shape[2]
    gu_chunk, dn_chunk = gu_stage.shape[2], dn_stage.shape[2]
    n_gu, n_dn = gu_rows // gu_chunk, ff // dn_chunk
    chunks = n_gu + n_dn

    def weight_part(c, owner):
        if c < n_gu:
            start = pl.multiple_of(owner * gu_rows + c * gu_chunk, 16)
            return gate_up.at[pl.ds(start, gu_chunk)]
        columns = pl.ds(pl.multiple_of(owner * dn_cols, 128), dn_cols)
        return down.at[pl.ds((c - n_gu) * dn_chunk, dn_chunk), columns]

    def staged(c):
        slot = c % 2
        if c < n_gu:
            part = pl.ds(c * gu_chunk, gu_chunk)
            refs = (gu_master, gu_moment, gu_grad)
            stages = (gu_stage.at[slot, 0], gu_stage.at[slot, 1], gu_grad_stage.at[slot])
        else:
            part = pl.ds((c - n_gu) * dn_chunk, dn_chunk)
            refs = (dn_master, dn_moment, dn_grad)
            stages = (dn_stage.at[slot, 0], dn_stage.at[slot, 1], dn_grad_stage.at[slot])
        return [
            pltpu.make_async_copy(ref.at[0, part], stage, stage_sem.at[c, i])
            for i, (ref, stage) in enumerate(zip(refs, stages))
        ]

    def prepare(first, last):
        for c in range(first, last):
            if c + 1 < chunks:
                for copy in staged(c + 1):
                    copy.start()
            for copy in staged(c):
                copy.wait()
            slot = c % 2
            mine = weight_part(c, g)
            if c < n_gu:
                mine[...] = updated(gu_stage[slot, 0], gu_stage[slot, 1], gu_grad_stage[slot])
            else:
                mine[...] = updated(dn_stage[slot, 0], dn_stage[slot, 1], dn_grad_stage[slot])
            for q in range(1, pairs):
                send(mine, mine, weight_send.at[c, q], weight_recv.at[c, q], same_core(q))
            send(mine, mine, weight_send.at[c, 0], weight_recv.at[c, 0], sibling)

    def relay(c):
        for q in range(1, pairs):
            owner = lax.rem(pair - q + pairs, pairs) * 2 + core
            part = weight_part(c, owner)
            arrive(part, weight_recv.at[c, q])
            k = pairs + q - 1
            send(part, part, weight_send.at[c, k], weight_recv.at[c, k], sibling)

    def from_sibling(c):
        arrive(weight_part(c, g + 1 - 2 * core), weight_recv.at[c, 0])

    def relayed(c):
        for q in range(1, pairs):
            owner = lax.rem(pair - q + pairs, pairs) * 2 + 1 - core
            arrive(weight_part(c, owner), weight_recv.at[c, pairs + q - 1])

    def select(table, source, outgoing):
        @pl.loop(0, width // TILE)
        def _(t):
            columns = pl.ds(pl.multiple_of(t * TILE, TILE), TILE)
            outgoing[:, columns] = jnp.dot(
                table[...], source[:, columns], preferred_element_type=jnp.float32
            ).astype(jnp.bfloat16)

    def hand_out_near(s):
        select(near_tab.at[s, 0], mixed.at[s], near_send.at[s])
        for j in range(1, half):
            send(
                near_send.at[s, seats(near(j))], slots.at[s, seats(me)],
                near_out_send.at[s, j], near_out_recv.at[s, me], near_device(near(j)),
            )
        pltpu.make_async_copy(
            near_send.at[s, seats(me)], slots.at[s, seats(me)], near_out_recv.at[s, me]
        ).start()

    def far_copies(s, b):
        origin = b * lines + line
        return [
            remote(
                far_send.at[b, s, seats(near(j))], slots.at[s, seats(origin, places)],
                far_out_send.at[b, s, j], far_out_recv.at[s, origin], near_device(near(j)),
            )
            for j in range(1, half)
        ]

    def hand_out_far(s):
        @pl.when(lands)
        def _():
            for b in range(2):
                origin = b * lines + line
                if s == 0:
                    arrive(relay_tab.at[b], tab_recv.at[b])
                arrive(far_rows.at[b, s], row_recv.at[b, s])
                select(relay_tab.at[b, s, 0], far_rows.at[b, s], far_send.at[b, s])
                for copy in far_copies(s, b):
                    copy.start()
                pltpu.make_async_copy(
                    far_send.at[b, s, seats(me)], slots.at[s, seats(origin, places)],
                    far_out_recv.at[s, origin],
                ).start()

        for b in range(2):
            landing_sends.append(functools.partial(far_copies, s, b))

    def project(s):
        for origin in range(half):
            arrive(slots.at[s, seats(origin)], near_out_recv.at[s, origin])
            arrive(slots.at[s, seats(origin, places)], far_out_recv.at[s, origin])

        @pl.loop(0, ff // 256)
        def _(t):
            left = pl.ds(pl.multiple_of(t * 256, 256), 256)
            right = pl.ds(pl.multiple_of(ff + t * 256, 256), 256)
            gate = jnp.dot(slots[s], gate_up[:, left], preferred_element_type=jnp.float32)
            up = jnp.dot(slots[s], gate_up[:, right], preferred_element_type=jnp.float32)
            hidden[:, left] = (gate / (1.0 + jnp.exp(-gate)) * up).astype(jnp.bfloat16)

    def far_return(s, q, y, b):
        columns = columns_of(q)
        return remote(
            slots.at[s, seats(b * lines + y, places), columns],
            far_back.at[b, s, seats(me), columns],
            far_back_send.at[s, q, b, y], far_back_recv.at[b, s, q, me], near_device(lander(y)),
        )

    def expand(s, q):
        @pl.loop(0, group // tile)
        def _(t):
            columns = tile_of(q, t)
            slots[s, :, columns] = jnp.dot(
                hidden[...], down[:, columns], preferred_element_type=jnp.float32
            ).astype(jnp.bfloat16)

        columns = columns_of(q)
        for y in range(lines):
            for b in range(2):
                other = me != lander(y)

                @pl.when(other)
                def _():
                    far_return(s, q, y, b).start()

                @pl.when(jnp.logical_not(other))
                def _():
                    pltpu.make_async_copy(
                        slots.at[s, seats(b * lines + y, places), columns_of(q)],
                        far_back.at[b, s, seats(me), columns_of(q)],
                        far_back_recv.at[b, s, q, me],
                    ).start()

                guarded_sends.append((other, functools.partial(far_return, s, q, y, b)))
        for j in range(1, half):
            send(
                slots.at[s, seats(near(j)), columns], near_back.at[s, seats(me), columns],
                near_back_send.at[s, q, j], near_back_recv.at[s, q, me], near_device(near(j)),
            )
        pltpu.make_async_copy(
            slots.at[s, seats(me), columns], near_back.at[s, seats(me), columns],
            near_back_recv.at[s, q, me],
        ).start()

    def weighted(table, back, columns):
        return lax.dot_general(
            table[...], back[:, columns], (((0,), (0,)), ((), ())),
            preferred_element_type=jnp.float32,
        )

    def part_copy(s, q, b):
        columns = columns_of(q)
        return remote(
            far_rows.at[b, s, :, columns], part_recv.at[s, :, columns],
            part_send_sem.at[b, s, q], part_recv_sem.at[s, q], source_device(b),
        )

    def part_copies(s, q, b):
        return [part_copy(s, q, b)]

    def sum_far(s, q):
        @pl.when(lands)
        def _():
            for b in range(2):
                for origin in range(half):
                    arrive(
                        far_back.at[b, s, seats(origin), columns_of(q)],
                        far_back_recv.at[b, s, q, origin],
                    )

                @pl.loop(0, group // tile)
                def _(t):
                    columns = tile_of(q, t)
                    far_rows[b, s, :, columns] = weighted(
                        relay_tab.at[b, s, 1], far_back.at[b, s], columns
                    ).astype(jnp.bfloat16)

                part_copy(s, q, b).start()

        for b in range(2):
            landing_sends.append(functools.partial(part_copies, s, q, b))

    def finish(s, q):
        for origin in range(half):
            arrive(near_back.at[s, seats(origin), columns_of(q)], near_back_recv.at[s, q, origin])
        arrive(part_recv.at[s, :, columns_of(q)], part_recv_sem.at[s, q])

        @pl.loop(0, group // tile)
        def _(t):
            columns = tile_of(q, t)
            total = weighted(near_tab.at[s, 1], near_back.at[s], columns)
            total = total + part_recv[s, :, columns].astype(jnp.float32)
            mixed[s, :, columns] = total.astype(jnp.bfloat16)

    for copy in staged(0):
        copy.start()
    prepare(0, n_gu // 2)
    own_copy.wait()
    for s in range(steps):
        hand_out_near(s)
    prepare(n_gu // 2, chunks)

    for c in range(n_gu // 2):
        relay(c)
    hand_out_far(0)
    for c in range(n_gu // 2, n_gu):
        relay(c)
    for c in range(n_gu):
        from_sibling(c)
        relayed(c)
    project(0)
    for c in range(n_gu, chunks):
        from_sibling(c)
    expand(0, 0)
    for s in range(1, steps):
        hand_out_far(s)
    for c in range(n_gu, chunks):
        relay(c)
    for c in range(n_gu, chunks):
        relayed(c)
    for q in range(1, pairs):
        expand(0, q)
    sum_far(0, 0)
    for s in range(1, steps):
        project(s)
        for q in range(pairs):
            expand(s, q)
    for s in range(steps):
        for q in range(pairs):
            if (s, q) != (0, 0):
                sum_far(s, q)
    for s in range(steps):
        for q in range(pairs):
            finish(s, q)

    for copy in sends:
        copy.wait_send()
    for other, build in guarded_sends:

        @pl.when(other)
        def _():
            build().wait_send()

    @pl.when(lands)
    def _():
        for build in landing_sends:
            for copy in build():
                copy.wait_send()


def per_device(
    tokens,
    expert_ids,
    route_gain,
    gate_up_master,
    gate_up_moment,
    gate_up_grad,
    down_master,
    down_moment,
    down_grad,
):
    steps, rows, top_k = expert_ids.shape
    width = tokens.shape[2]
    n_engine, n_expert = lax.axis_size("engine"), lax.axis_size("expert")
    half, pairs = n_expert // 2, n_engine // 2
    cap = 3 * rows * top_k // (2 * n_expert)
    cap = -(-cap // 16) * 16
    places = half * cap
    ff = down_master.shape[1]

    named = expert_ids[:, None, :, :] == jnp.arange(n_expert, dtype=jnp.int32)[None, :, None, None]
    share = (route_gain / jnp.sum(route_gain, axis=2, keepdims=True)).astype(jnp.bfloat16)
    chosen = jnp.any(named, axis=3)
    portion = jnp.sum(jnp.where(named, share[:, None].astype(jnp.float32), 0.0), axis=3)
    ahead = jnp.arange(rows)[:, None] < jnp.arange(rows)[None, :]
    place = jnp.einsum(
        "ser,rq->seq", chosen.astype(jnp.bfloat16), ahead.astype(jnp.bfloat16),
        preferred_element_type=jnp.float32,
    ).astype(jnp.int32)
    match = chosen[:, :, None, :] & (
        place[:, :, None, :] == jnp.arange(cap, dtype=jnp.int32)[None, None, :, None]
    )
    table = jnp.stack(
        [match.astype(jnp.bfloat16), jnp.where(match, portion[:, :, None, :], 0.0).astype(jnp.bfloat16)],
        axis=1,
    ).reshape(steps, 2, 2, places, rows)
    side = lax.axis_index("expert") // half
    near_tab = lax.dynamic_index_in_dim(table, side, 2, keepdims=False)
    far_tab = lax.dynamic_index_in_dim(table, 1 - side, 2, keepdims=False)

    gu_rows, dn_cols = gate_up_master.shape[1], down_master.shape[2]
    gu_chunk, dn_chunk = min(128, gu_rows // 4), ff // 8
    chunks = gu_rows // gu_chunk + 8
    lines = half // 2
    bf16, f32 = jnp.bfloat16, jnp.float32
    dma = pltpu.SemaphoreType.DMA
    hbm, vmem = pl.BlockSpec(memory_space=pl.ANY), pl.BlockSpec(memory_space=pltpu.VMEM)
    return pl.pallas_call(
        functools.partial(layer_kernel, n_engine, n_expert, cap),
        out_shape=jax.ShapeDtypeStruct(tokens.shape, bf16),
        in_specs=[hbm, vmem, vmem] + [hbm] * 6,
        out_specs=vmem,
        scratch_shapes=[
            pltpu.VMEM((width, 2 * ff), bf16),
            pltpu.VMEM((ff, width), bf16),
            pltpu.VMEM((2, steps, rows, width), bf16),
            pltpu.VMEM((2, steps, 2, places, rows), bf16),
            pltpu.VMEM((steps, places, width), bf16),
            pltpu.VMEM((2, steps, places, width), bf16),
            pltpu.VMEM((steps, 2 * places, width), bf16),
            pltpu.VMEM((2 * places, ff), bf16),
            pltpu.VMEM((steps, places, width), bf16),
            pltpu.VMEM((2, steps, places, width), bf16),
            pltpu.VMEM((steps, rows, width), bf16),
            pltpu.VMEM((2, 2, gu_chunk, 2 * ff), f32),
            pltpu.VMEM((2, gu_chunk, 2 * ff), bf16),
            pltpu.VMEM((2, 2, dn_chunk, dn_cols), f32),
            pltpu.VMEM((2, dn_chunk, dn_cols), bf16),
            dma((1,)),
            dma((chunks, 3)),
            dma((1,)),
            dma((2,)),
            dma((steps,)),
            dma((2, steps)),
            dma((steps, half)),
            dma((steps, half)),
            dma((2, steps, half)),
            dma((steps, half)),
            dma((steps, pairs, half)),
            dma((steps, pairs, half)),
            dma((steps, pairs, 2, lines)),
            dma((2, steps, pairs, half)),
            dma((2, steps, pairs)),
            dma((steps, pairs)),
            dma((chunks, 2 * pairs - 1)),
            dma((chunks, 2 * pairs - 1)),
        ],
        compiler_params=pltpu.CompilerParams(
            collective_id=0, has_side_effects=True, vmem_limit_bytes=63 * 1024 * 1024
        ),
    )(
        tokens, near_tab, far_tab, gate_up_master, gate_up_moment, gate_up_grad,
        down_master, down_moment, down_grad,
    )


def solution(mesh):
    return jax.shard_map(
        per_device,
        mesh=mesh,
        in_specs=(
            P(None, ("engine", "expert"), None),
            P(None, ("engine", "expert"), None),
            P(None, ("engine", "expert"), None),
            P("expert", "engine", None),
            P("expert", "engine", None),
            P("expert", "engine", None),
            P("expert", None, "engine"),
            P("expert", None, "engine"),
            P("expert", None, "engine"),
        ),
        out_specs=P(None, ("engine", "expert"), None),
        check_vma=False,
    )
```

time: 265 us -> 260 us (0.981)
  the two profiles are of different devices: /device:TPU:5 before, /device:TPU:30 now
where the time goes in v2:
time: 260 us; the launch traced here: 259 us
  Pallas kernels  253 us (97%)
  local copies, waits for them, and re-layouts  4.09 us (2%)
    pallas_call x1, Pallas kernels, per_device(): pl.pallas_call(functools.partial(layer_kernel, n_engine, n_expert, cap),...  253 us

profile of v2, /device:TPU:30, one launch (start us, length us, event | category | flops | bytes accessed | tf_op | source)
XLA Modules:
  0.0 259.5 jit_solution(8586775315190974997)
XLA Ops:
  0.0 0.7 fusion.8
  0.7 0.8 fusion.3
  1.5 0.7 select_reduce_fusion
  2.2 0.1 eq.51
  2.2 0.1 convolution_convert_fusion
  2.5 0.2 select_convert_fusion
  2.8 0.8 copy_bitcast_fusion
  3.6 252.8 %shard_map.91 = bf16[2,128,4096]{2,1,0:T(8,128)(2,1)} custom-call(bf16[2,128,4096]{2,1,0:T(8,128)(2,1)} %tokens.1, bf16[2,2,192,128]{3,2,1,0:T(8,128)(2,1)} %get-tuple-element.10.near_tab, bf16[2,2,192,128]{3,2,1,0:T(8,128)(2,1)} %get-tuple-element.9.far_tab, f32[1,1024,1536]{2,1,0:T(8,128)} %gu_master.1, f32[1,1024,1536]{2,1,0:T(8,128)} %gu_moment.1, ...), custom_call_target="tpu_custom_call" | custom-call | tf_op jit(solution)/shard_map/pallas_call | solution.py:459
  256.3 3.1 %copy.21 = bf16[2,128,4096]{2,1,0:T(8,128)(2,1)} copy(bf16[2,128,4096]{2,1,0:T(8,128)(2,1)} %shard_map.91) | data formatting | bytes 4194304
  (6 shorter events, 0.2 us)
